TPU v7x, 256 devices: a whole 4x4x8 slice. The times are simulated.
256 devices in a mesh: inner: 16 (over z_hi, y), outer: 16 (over x, z_lo, core).
Axes of the slice: x: 4, y: 4, z: 8 (z_hi: 4, z_lo: 2; z = z_hi * 2 + z_lo), core: 2. Of those that a mesh axis runs over, the one named last changes fastest.
Arguments:
- frames: bfloat16 [16, 96, 64, 2048], P('outer', 'inner'), may hold values from -6 to 6
- queries: bfloat16 [16, 96, 64, 1024], P('outer', 'inner'), may hold values from -160 to 160
- w_keyval: bfloat16 [2048, 2048], replicated, may hold values from -0.125 to 0.125
- bucket_table: int32 [54], replicated, may hold values from 0 to 31
- bias_table: float32 [32, 8], replicated, may hold values from -4 to 4
- block_mask: int32 [16, 16, 9], P('outer', 'inner'), may hold values 0 or 1
Outputs:
- attended: bfloat16 [16, 96, 64, 1024], P('outer', 'inner')
All inputs are finite; a program needn't handle non-finite values. No bound on the sum of `block_mask` on one device may be relied on, other than what follows from the above.
Results may differ from a plain program's by a relative error of at most 0.011.
Values may be sent and summed in bfloat16 or wider, within the bound.
No kernel may reach another device: no remote copies, remote signals or barrier semaphores. Data moves between devices by JAX's collectives and lax.ppermute only.
A program may use at most 192 MiB of HBM per device.

v0:
```python
import jax
import jax.numpy as jnp
from jax import lax
from jax.experimental import pallas as pl
from jax.experimental.pallas import tpu as pltpu
from jax.sharding import PartitionSpec as P

SPAN = 8
HEAD = 128
HEADS = 8
ROWS = 8
GROUP = 64
FR = 6
CHUNK = SPAN * FR
KEYS = 128
MESSAGE = 3 * CHUNK + ROWS
PIECE = 16
SLABS = 4
NEG = -1e30
VMEM = pl.BlockSpec(memory_space=pltpu.VMEM)
SMEM = pl.BlockSpec(memory_space=pltpu.SMEM)


def swap_matrix(frames, rows, back):
    size = frames * rows
    a = lax.broadcasted_iota(jnp.int32, (size, size), 1 if back else 0)
    b = lax.broadcasted_iota(jnp.int32, (size, size), 0 if back else 1)
    hit = b == (a % frames) * rows + a // frames
    return jnp.where(hit, 1.0, 0.0).astype(jnp.bfloat16)


def block_number():
    return lax.axis_index("inner") * lax.axis_size("outer") + lax.axis_index("outer")


def prep_kernel(
    mask_hbm, x_hbm, w_hbm, q_hbm, out_hbm, mask_ref, x, w, q, total, out_ref, mask_sem, x_sem, w_sem, q_sem, out_sem
):
    depth = w.shape[0] // SLABS
    loads = []
    for slab in range(SLABS):
        span = slice(slab * depth, (slab + 1) * depth)
        loads.append(
            (
                pltpu.make_async_copy(w_hbm.at[span], w.at[span], w_sem.at[slab]),
                pltpu.make_async_copy(x_hbm.at[:, span], x.at[:, span], x_sem.at[slab]),
            )
        )
    q_load = pltpu.make_async_copy(q_hbm, q, q_sem)
    mask_load = pltpu.make_async_copy(mask_hbm, mask_ref, mask_sem)
    for load in loads[0] + loads[1]:
        load.start()
    mask_load.start()
    spatial = x.shape[0] // FR

    def place(part, pair, n):
        for half in range(2):
            cols = slice(half * HEAD, (half + 1) * HEAD)
            for group in range(spatial // ROWS):
                at = [f * spatial + group * ROWS for f in range(FR)]
                rows = jnp.concatenate([part[a : a + ROWS, cols] for a in at], axis=0)
                out_ref[group, 2 * pair + half, n * CHUNK : (n + 1) * CHUNK, :] = rows.astype(jnp.bfloat16)

    block = block_number()
    key = lax.broadcasted_iota(jnp.int32, (2 * ROWS, KEYS), 1) - (KEYS - CHUNK)
    reach = block % SPAN - (key + 96 * FR) // FR + 96
    seen = jnp.where(reach == 0, 1.0, 0.0)
    mask_load.wait()
    for m in range(1, SPAN + 1):
        visible = jnp.where((mask_ref[m] == 1) & (block >= m), 1.0, 0.0)
        seen = jnp.where(reach == m, visible, seen)
    seen = seen.astype(jnp.bfloat16)[0:ROWS]
    for group in range(spatial // ROWS):
        for head in range(HEADS):
            out_ref[group, head, 3 * CHUNK :, :] = seen

    for slab in range(SLABS):
        for load in loads[slab]:
            load.wait()
        if slab + 2 < SLABS:
            for load in loads[slab + 2]:
                load.start()
        if slab == 0:
            q_load.start()
        if slab == SLABS - 1:
            q_load.wait()
            for pair in range(HEADS // 2):
                place(q[:, pair * 2 * HEAD : (pair + 1) * 2 * HEAD].astype(jnp.float32), pair, 2)
        span = slice(slab * depth, (slab + 1) * depth)
        stores = []
        for pair in range(HEADS // 2):
            for n in range(2):
                first = (n * HEADS + 2 * pair) * HEAD
                cols = slice(first, first + 2 * HEAD)
                part = jnp.dot(x[:, span], w[span, cols], preferred_element_type=jnp.float32)
                if slab > 0:
                    part = part + total[:, cols]
                if slab < SLABS - 1:
                    total[:, cols] = part
                else:
                    place(part, pair, n)
            if slab == SLABS - 1:
                heads = slice(2 * pair, 2 * pair + 2)
                store = pltpu.make_async_copy(out_ref.at[:, heads], out_hbm.at[:, heads], out_sem.at[pair])
                store.start()
                stores.append(store)
    for store in stores:
        store.wait()


def prep(frames, queries, w_keyval, block_mask):
    tokens, width = frames.shape
    groups = tokens // FR // ROWS
    any_ = pl.BlockSpec(memory_space=pl.ANY)
    return pl.pallas_call(
        prep_kernel,
        in_specs=[any_] * 4,
        out_specs=any_,
        out_shape=jax.ShapeDtypeStruct((groups, HEADS, MESSAGE, HEAD), jnp.bfloat16),
        scratch_shapes=[
            pltpu.SMEM(block_mask.shape, block_mask.dtype),
            pltpu.VMEM(frames.shape, jnp.bfloat16),
            pltpu.VMEM(w_keyval.shape, jnp.bfloat16),
            pltpu.VMEM(queries.shape, jnp.bfloat16),
            pltpu.VMEM((tokens, w_keyval.shape[1]), jnp.float32),
            pltpu.VMEM((groups, HEADS, MESSAGE, HEAD), jnp.bfloat16),
            pltpu.SemaphoreType.DMA,
            pltpu.SemaphoreType.DMA((SLABS,)),
            pltpu.SemaphoreType.DMA((SLABS,)),
            pltpu.SemaphoreType.DMA,
            pltpu.SemaphoreType.DMA((HEADS // 2,)),
        ],
        compiler_params=pltpu.CompilerParams(vmem_limit_bytes=58 * 1024 * 1024),
        name="prep",
    )(block_mask, frames, w_keyval, queries)


def bias_of_head(bucket_ref, table_ref):
    head = block_number() % HEADS
    i = lax.broadcasted_iota(jnp.int32, (CHUNK, KEYS), 0)
    key = lax.broadcasted_iota(jnp.int32, (CHUNK, KEYS), 1) - (KEYS - CHUNK)
    off = i - key
    bias = jnp.full((CHUNK, KEYS), NEG, jnp.float32)
    for d in range(bucket_ref.shape[0]):
        bias = jnp.where(off == d, table_ref[head, bucket_ref[d]], bias)
    reach = i // FR - (key + 96 * FR) // FR + 96
    return jnp.where((reach >= 0) & (reach <= SPAN), bias, NEG)


def chunk_bias(base, rows):
    i = lax.broadcasted_iota(jnp.int32, (CHUNK, SPAN * ROWS), 0)
    b = lax.broadcasted_iota(jnp.int32, (CHUNK, SPAN * ROWS), 1)
    spread = jnp.where(i // FR * ROWS == b, 1.0, 0.0).astype(jnp.bfloat16)
    rows = rows.astype(jnp.float32).reshape(SPAN * ROWS, KEYS).astype(jnp.bfloat16)
    seen = jnp.dot(spread, rows, preferred_element_type=jnp.float32)
    return jnp.where(seen > 0.5, base, NEG)


def attend(held, start, bias):
    first = start + CHUNK - KEYS
    scores = [
        lax.dot_general(
            held[s, start : start + CHUNK, 2 * HEAD :],
            held[s, first : first + KEYS, 0:HEAD],
            (((1,), (1,)), ((), ())),
            preferred_element_type=jnp.float32,
        )
        for s in range(ROWS)
    ]
    scores = jnp.stack(scores, axis=0) * (HEAD**-0.5) + bias[None]
    expo = jnp.exp(scores - jnp.max(scores, axis=2, keepdims=True))
    weights = expo * (1.0 / jnp.sum(expo, axis=2, keepdims=True))
    weights = weights.astype(jnp.bfloat16)
    return [
        jnp.dot(
            weights[s], held[s, first : first + KEYS, HEAD : 2 * HEAD], preferred_element_type=jnp.float32
        ).astype(jnp.bfloat16)
        for s in range(ROWS)
    ]


def turn_in(held, swap, got_ref, blocks, parts, at):
    rows = [
        got_ref[blocks, n * CHUNK : (n + 1) * CHUNK, :].reshape(CHUNK * ROWS, HEAD) for n in range(parts)
    ]
    rows = jnp.concatenate(rows, axis=1)
    for piece in range(CHUNK // PIECE):
        part = rows[piece * PIECE * ROWS : (piece + 1) * PIECE * ROWS]
        turned = jnp.dot(swap, part, preferred_element_type=jnp.float32).astype(jnp.bfloat16)
        start = at + piece * PIECE
        held[:, start : start + PIECE, 0 : parts * HEAD] = turned.reshape(ROWS, PIECE, parts * HEAD)


def turn_out(out_ref, back, mixed, at):
    for piece in range(CHUNK // PIECE):
        rows = [m[piece * PIECE : (piece + 1) * PIECE] for m in mixed]
        rows = jnp.concatenate(rows, axis=0)
        start = at + piece * PIECE * ROWS
        out_ref[start : start + PIECE * ROWS, :] = jnp.dot(
            back, rows, preferred_element_type=jnp.float32
        ).astype(jnp.bfloat16)


def main_kernel(bucket_ref, table_ref, got_ref, out_ref, bias_ref, first_ref, held):
    base = bias_of_head(bucket_ref, table_ref)
    swap = swap_matrix(PIECE, ROWS, False)
    back = swap_matrix(PIECE, ROWS, True)
    lead = CHUNK
    held[:, 0:lead, :] = jnp.zeros((ROWS, lead, 3 * HEAD), jnp.bfloat16)
    for chunk in range(GROUP // SPAN):
        blocks = slice(chunk * SPAN, (chunk + 1) * SPAN)
        at = lead + chunk * CHUNK
        turn_in(held, swap, got_ref, blocks, 3, at)
        bias = chunk_bias(base, got_ref[blocks, 3 * CHUNK :, :])
        if chunk > 0:
            turn_out(out_ref, back, attend(held, at, bias), chunk * CHUNK * ROWS)
        else:
            bias_ref[...] = bias
            first_ref[:, : KEYS - CHUNK, :] = jnp.zeros((ROWS, KEYS - CHUNK, 3 * HEAD), jnp.bfloat16)
            first_ref[:, KEYS - CHUNK :, :] = held[:, at : at + CHUNK, :]


def main_part(bucket_table, bias_table, got):
    frames = GROUP * FR
    return pl.pallas_call(
        main_kernel,
        in_specs=[SMEM, SMEM, VMEM],
        out_specs=[VMEM] * 3,
        out_shape=[
            jax.ShapeDtypeStruct((frames * ROWS, HEAD), jnp.bfloat16),
            jax.ShapeDtypeStruct((CHUNK, KEYS), jnp.float32),
            jax.ShapeDtypeStruct((ROWS, KEYS, 3 * HEAD), jnp.bfloat16),
        ],
        scratch_shapes=[pltpu.VMEM((ROWS, CHUNK + frames, 3 * HEAD), jnp.bfloat16)],
        compiler_params=pltpu.CompilerParams(vmem_limit_bytes=40 * 1024 * 1024),
        cost_estimate=pl.CostEstimate(flops=2_000_000_000, bytes_accessed=16_000_000, transcendentals=0),
        name="main_part",
    )(bucket_table, bias_table, got)


def first_kernel(bias_ref, halo_ref, own_ref, rest_ref, out_ref, held):
    swap = swap_matrix(PIECE, ROWS, False)
    back = swap_matrix(PIECE, ROWS, True)
    turn_in(held, swap, halo_ref, slice(0, SPAN), 2, KEYS - 2 * CHUNK)
    turn_out(out_ref, back, attend(held, KEYS - CHUNK, bias_ref[...]), 0)


def first_part(bias, halo, own, rest):
    return pl.pallas_call(
        first_kernel,
        in_specs=[VMEM] * 4,
        out_specs=[VMEM] * 2,
        out_shape=[jax.ShapeDtypeStruct(a.shape, a.dtype) for a in (rest, own)],
        input_output_aliases={2: 1, 3: 0},
        compiler_params=pltpu.CompilerParams(vmem_limit_bytes=40 * 1024 * 1024),
        name="first_part",
    )(bias, halo, own, rest)[0]


def exchange(array, groups):
    return lax.all_to_all(array, ("inner", "outer"), 0, 0, tiled=True, axis_index_groups=groups)


def on_device(frames, queries, w_keyval, bucket_table, bias_table, block_mask):
    n_outer = lax.axis_size("outer")
    n_blocks = lax.axis_size("inner") * n_outer
    groups = [list(range(g, g + GROUP)) for g in range(0, n_blocks, GROUP)]
    spatial, width = frames.shape[2:]

    sent = prep(
        frames.reshape(-1, width),
        queries.reshape(-1, queries.shape[3]),
        w_keyval,
        block_mask.reshape(-1),
    )
    got = exchange(sent.reshape(GROUP, MESSAGE, HEAD), groups)
    perm = [(i, i + GROUP) for i in range(n_blocks - GROUP)]
    halo = lax.ppermute(got[GROUP - SPAN :, : 2 * CHUNK, :], ("inner", "outer"), perm)
    rest, bias, own = main_part(bucket_table, bias_table.T, got)
    mixed = first_part(bias, halo, own, rest)
    out = exchange(mixed.reshape(GROUP, CHUNK, HEAD), groups)
    out = out.reshape(spatial // ROWS, HEADS, FR, ROWS, HEAD)
    return out.transpose(2, 0, 3, 1, 4).reshape(queries.shape)


def solution(mesh):
    in_specs = (
        P("outer", "inner", None, None),
        P("outer", "inner", None, None),
        P(),
        P(),
        P(),
        P("outer", "inner", None),
    )
    out_specs = P("outer", "inner", None, None)
    return jax.shard_map(
        on_device, mesh=mesh, in_specs=in_specs, out_specs=out_specs, check_vma=False
    )
```

profile of v0, /device:TPU:1, one launch (start us, length us, event | category | flops | bytes accessed | tf_op | source)
XLA Modules:
  0.0 86.7 jit_solution(4169652148917533799)
XLA Ops:
  0.0 6.5 %prep.1 = bf16[8,8,152,128]{3,2,1,0:T(8,128)(2,1)} custom-call(s32[9]{0:T(128)} %bitcast.18, bf16[384,2048]{1,0:T(8,128)(2,1)} %bitcast.16, bf16[2048,2048]{1,0:T(8,128)(2,1)} %w_hbm.1, bf16[384,1024]{1,0:T(8,128)(2,1)} %bitcast.17), custom_call_target="tpu_custom_call" | custom-call | tf_op jit(solution)/shard_map/prep/pallas_call | solution.py:115
  6.5 0.0 copy-start
  6.5 0.0 copy-start.1
  6.6 44.2 %all_to_all.10.got_ref = bf16[64,152,128]{2,1,0:T(8,128)(2,1)S(1)} all-to-all(bf16[64,152,128]{2,1,0:T(8,128)(2,1)} %bitcast.14), channel_id=1, replica_groups={{0,1,2,3,4,5,6,7,8,9,10,11,12,13,14,15,16,17,18,19,20,21,22,23,24,25,26..., dimensions={0} | all-to-all | bytes 4980736 | tf_op jit(solution)/shard_map/all_to_all | solution.py:261
  50.8 4.9 %collective-permute-start = (bf16[8,96,128]{2,1,0:T(8,128)(2,1)S(1)}, bf16[8,96,128]{2,1,0:T(8,128)(2,1)S(1)}, u32[]{:S(2)}, u32[]{:S(2)}) collective-permute-start(bf16[8,96,128]{2,1,0:T(8,128)(2,1)S(1)} %slice.4), channel_id=1, source_target_pairs={{0,64},{1,65},{2,66},{3,67},{4,68},{5,69},{6,70},{7,71},{8,72},{9,... | collective-permute-start | bytes 589832 | tf_op jit(solution)/shard_map/ppermute | solution.py:278
  55.7 0.0 copy-done
  55.7 0.0 copy-done.1
  55.7 6.3 %main_part.1 = (bf16[3072,128]{1,0:T(8,128)(2,1)S(1)}, f32[48,128]{1,0:T(8,128)S(1)}, bf16[8,128,384]{2,1,0:T(8,128)(2,1)S(1)}) custom-call(s32[54]{0:T(128)S(1)} %copy-done.1, f32[8,32]{1,0:T(8,128)S(1)} %bitcast.13, bf16[64,152,128]{2,1,0:T(8,128)(2,1)S(1)} %all_to_all.10.got_ref), custom_call_target="tpu_custom_call" | custom-call | flops 2000000000 | bytes 16000000 | tf_op jit(solution)/shard_map/main_part/pallas_call | solution.py:225
  62.1 0.0 collective-permute-done.halo_ref
  62.1 0.9 %first_part.1 = (bf16[3072,128]{1,0:T(8,128)(2,1)S(1)}, bf16[8,128,384]{2,1,0:T(8,128)(2,1)S(1)}) custom-call(f32[48,128]{1,0:T(8,128)S(1)} %get-tuple-element.9.bias_ref, bf16[8,96,128]{2,1,0:T(8,128)(2,1)S(1)} %collective-permute-done.halo_ref, bf16[8,128,384]{2,1,0:T(8,128)(2,1)S(1)} %get-tuple-element.10.own_ref, ...), custom_call_target="tpu_custom_call", output_to_operand_aliasing={{1}: (2, {}), {0}: (3, {})} | custom-call | tf_op jit(solution)/shard_map/first_part/pallas_call | solution.py:249
  63.0 22.6 %all_to_all.11 = bf16[64,48,128]{2,1,0:T(8,128)(2,1)S(1)} all-to-all(bf16[64,48,128]{2,1,0:T(8,128)(2,1)S(1)} %bitcast.12), channel_id=1, replica_groups={{0,1,2,3,4,5,6,7,8,9,10,11,12,13,14,15,16,17,18,19,20,21,22,23,24,25,26..., dimensions={0} | all-to-all | bytes 1572864 | tf_op jit(solution)/shard_map/all_to_all | solution.py:261
  85.6 1.1 %copy.11 = bf16[8,8,6,8,128]{4,3,1,0,2:T(8,128)(2,1)} copy(bf16[8,8,6,8,128]{4,3,2,1,0:T(8,128)(2,1)S(1)} %bitcast.15) | data formatting | bytes 1572864 | tf_op jit(solution)/shard_map/reshape | solution.py:282
  (1 shorter events, 0.0 us)
Async XLA Ops:
  6.5 49.2 %copy-start = (f32[32,8]{0,1:T(8,128)S(1)}, f32[32,8]{0,1:T(8,128)}, u32[]{:S(2)}) copy-start(f32[32,8]{0,1:T(8,128)} %param.10) | copy-start | bytes 3076
  6.5 49.2 %copy-start.1 = (s32[54]{0:T(128)S(1)}, s32[54]{0:T(128)}, u32[]{:S(2)}) copy-start(s32[54]{0:T(128)} %bucket_ref.1) | copy-start | bytes 652
  50.8 11.3 %collective-permute-start = (bf16[8,96,128]{2,1,0:T(8,128)(2,1)S(1)}, bf16[8,96,128]{2,1,0:T(8,128)(2,1)S(1)}, u32[]{:S(2)}, u32[]{:S(2)}) collective-permute-start(bf16[8,96,128]{2,1,0:T(8,128)(2,1)S(1)} %slice.4), channel_id=1, source_target_pairs={{0,64},{1,65},{2,66},{3,67},{4,68},{5,69},{6,70},{7,71},{8,72},{9,... | collective-permute-start | bytes 589832 | tf_op jit(solution)/shard_map/ppermute | solution.py:278
where the time goes:
time: 86.9 us; the launch traced here: 86.7 us
  blocking collectives  66.8 us (77%)
  Pallas kernels  13.8 us (16%)
  starting transfers between devices  4.91 us (6%)
  local copies, waits for them, and re-layouts  1.13 us (1%)
    all_to_all x2, blocking collectives, exchange(): lax.all_to_all(array, ('inner', 'outer'), 0, 0, tiled=True, axis_index_gr...  66.8 us
    pallas_call x1, Pallas kernels, prep(): pl.pallas_call(prep_kernel, in_specs=[any_] * 4, out_specs=any_, out_shap...  6.53 us
    pallas_call x1, Pallas kernels, main_part(): pl.pallas_call(main_kernel, in_specs=[SMEM, SMEM, VMEM], out_specs=[VMEM]...  6.35 us
    ppermute x1, starting transfers between devices, on_device(): lax.ppermute(got[GROUP - SPAN:, :2 * CHUNK, :], ('inner', 'outer'), perm)  4.91 us
  transfers between devices with their start and end apart: 1, of which 0 were waited for; matrix products, arithmetic and copies ran while one was open for 0% of the time, Pallas kernels for 7%

commit v1 on v0

--- a/solution.py
+++ b/solution.py
@@ -156,27 +156,33 @@
     return jnp.where(seen > 0.5, base, NEG)
 
 
-def attend(held, start, bias):
+def score(held, start, bias):
     first = start + CHUNK - KEYS
-    scores = [
-        lax.dot_general(
-            held[s, start : start + CHUNK, 2 * HEAD :],
-            held[s, first : first + KEYS, 0:HEAD],
-            (((1,), (1,)), ((), ())),
-            preferred_element_type=jnp.float32,
-        )
-        for s in range(ROWS)
-    ]
-    scores = jnp.stack(scores, axis=0) * (HEAD**-0.5) + bias[None]
+    scores = []
+    for s in range(0, ROWS, 2):
+        q = jnp.concatenate([held[t, start : start + CHUNK, 2 * HEAD :] for t in (s, s + 1)], axis=0)
+        k = jnp.concatenate([held[t, first : first + KEYS, 0:HEAD] for t in (s, s + 1)], axis=0)
+        both = lax.dot_general(q, k, (((1,), (1,)), ((), ())), preferred_element_type=jnp.float32)
+        scores += [both[0:CHUNK, 0:KEYS], both[CHUNK:, KEYS:]]
+    return jnp.stack(scores, axis=0) * (HEAD**-0.5) + bias[None]
+
+
+def mix(held, start, scores):
+    first = start + CHUNK - KEYS
     expo = jnp.exp(scores - jnp.max(scores, axis=2, keepdims=True))
     weights = expo * (1.0 / jnp.sum(expo, axis=2, keepdims=True))
     weights = weights.astype(jnp.bfloat16)
-    return [
-        jnp.dot(
-            weights[s], held[s, first : first + KEYS, HEAD : 2 * HEAD], preferred_element_type=jnp.float32
-        ).astype(jnp.bfloat16)
-        for s in range(ROWS)
-    ]
+    mixed = []
+    for s in range(0, ROWS, 2):
+        v = jnp.concatenate([held[t, first : first + KEYS, HEAD : 2 * HEAD] for t in (s, s + 1)], axis=1)
+        both = jnp.dot(weights[s : s + 2].reshape(2 * CHUNK, KEYS), v, preferred_element_type=jnp.float32)
+        both = both.astype(jnp.bfloat16)
+        mixed += [both[0:CHUNK, 0:HEAD], both[CHUNK:, HEAD:]]
+    return mixed
+
+
+def attend(held, start, bias):
+    return mix(held, start, score(held, start, bias))
 
 
 def turn_in(held, swap, got_ref, blocks, parts, at):
@@ -208,16 +214,26 @@
     lead = CHUNK
     held[:, 0:lead, :] = jnp.zeros((ROWS, lead, 3 * HEAD), jnp.bfloat16)
     for chunk in range(GROUP // SPAN):
-        blocks = slice(chunk * SPAN, (chunk + 1) * SPAN)
-        at = lead + chunk * CHUNK
-        turn_in(held, swap, got_ref, blocks, 3, at)
-        bias = chunk_bias(base, got_ref[blocks, 3 * CHUNK :, :])
-        if chunk > 0:
-            turn_out(out_ref, back, attend(held, at, bias), chunk * CHUNK * ROWS)
-        else:
-            bias_ref[...] = bias
-            first_ref[:, : KEYS - CHUNK, :] = jnp.zeros((ROWS, KEYS - CHUNK, 3 * HEAD), jnp.bfloat16)
-            first_ref[:, KEYS - CHUNK :, :] = held[:, at : at + CHUNK, :]
+        turn_in(held, swap, got_ref, slice(chunk * SPAN, (chunk + 1) * SPAN), 3, lead + chunk * CHUNK)
+
+    def bias_of(chunk):
+        return chunk_bias(base, got_ref[chunk * SPAN : (chunk + 1) * SPAN, 3 * CHUNK :, :])
+
+    bias_ref[...] = bias_of(0)
+    first_ref[:, : KEYS - CHUNK, :] = jnp.zeros((ROWS, KEYS - CHUNK, 3 * HEAD), jnp.bfloat16)
+    first_ref[:, KEYS - CHUNK :, :] = held[:, lead : lead + CHUNK, :]
+    chunks = GROUP // SPAN
+    scores = score(held, lead + CHUNK, bias_of(1))
+    mixed = None
+    for chunk in range(1, chunks):
+        after = None
+        if chunk + 1 < chunks:
+            after = score(held, lead + (chunk + 1) * CHUNK, bias_of(chunk + 1))
+        if mixed is not None:
+            turn_out(out_ref, back, mixed, (chunk - 1) * CHUNK * ROWS)
+        mixed = mix(held, lead + chunk * CHUNK, scores)
+        scores = after
+    turn_out(out_ref, back, mixed, (chunks - 1) * CHUNK * ROWS)
 
 
 def main_part(bucket_table, bias_table, got):

time: 86.9 us -> 86.9 us (level)
  Pallas kernels: 13.8 us -> 10.8 us
  blocking collectives: 66.8 us -> 69.3 us
    pallas_call x1, Pallas kernels: 6.35 us -> 3.38 us  [main_part(): pl.pallas_call(main_kernel, in_specs=[SMEM, SMEM, VMEM], out_specs=[VMEM]...]
    all_to_all x2, blocking collectives: 66.8 us -> 69.3 us  [exchange(): lax.all_to_all(array, ('inner', 'outer'), 0, 0, tiled=True, axis_index_gr...]
  transfers between devices with their start and end apart: 1 -> 1, of which waited for: 0 -> 1; matrix products, arithmetic and copies ran while one was open for 0% -> 0% of each run, Pallas kernels for 7% -> 4%
where the time goes in v1:
time: 86.9 us; the launch traced here: 86.6 us
  blocking collectives  69.3 us (80%)
  Pallas kernels  10.8 us (12%)
  starting transfers between devices  4.91 us (6%)
  local copies, waits for them, and re-layouts  1.13 us (1%)
    all_to_all x2, blocking collectives, exchange(): lax.all_to_all(array, ('inner', 'outer'), 0, 0, tiled=True, axis_index_gr...  69.3 us
    pallas_call x1, Pallas kernels, prep(): pl.pallas_call(prep_kernel, in_specs=[any_] * 4, out_specs=any_, out_shap...  6.53 us
    ppermute x1, starting transfers between devices, on_device(): lax.ppermute(got[GROUP - SPAN:, :2 * CHUNK, :], ('inner', 'outer'), perm)  4.91 us
    pallas_call x1, Pallas kernels, main_part(): pl.pallas_call(main_kernel, in_specs=[SMEM, SMEM, VMEM], out_specs=[VMEM]...  3.38 us
  transfers between devices with their start and end apart: 1, of which 1 were waited for; matrix products, arithmetic and copies ran while one was open for 0% of the time, Pallas kernels for 4%

profile of v1, /device:TPU:1, one launch (start us, length us, event | category | flops | bytes accessed | tf_op | source)
XLA Modules:
  0.0 86.6 jit_solution(14242926401141134068)
XLA Ops:
  0.0 6.5 %prep.1 = bf16[8,8,152,128]{3,2,1,0:T(8,128)(2,1)} custom-call(s32[9]{0:T(128)} %bitcast.18, bf16[384,2048]{1,0:T(8,128)(2,1)} %bitcast.16, bf16[2048,2048]{1,0:T(8,128)(2,1)} %w_hbm.1, bf16[384,1024]{1,0:T(8,128)(2,1)} %bitcast.17), custom_call_target="tpu_custom_call" | custom-call | tf_op jit(solution)/shard_map/prep/pallas_call | solution.py:115
  6.5 0.0 copy-start
  6.5 0.0 copy-start.1
  6.6 44.2 %all_to_all.10.got_ref = bf16[64,152,128]{2,1,0:T(8,128)(2,1)S(1)} all-to-all(bf16[64,152,128]{2,1,0:T(8,128)(2,1)} %bitcast.14), channel_id=1, replica_groups={{0,1,2,3,4,5,6,7,8,9,10,11,12,13,14,15,16,17,18,19,20,21,22,23,24,25,26..., dimensions={0} | all-to-all | bytes 4980736 | tf_op jit(solution)/shard_map/all_to_all | solution.py:277
  50.8 4.9 %collective-permute-start = (bf16[8,96,128]{2,1,0:T(8,128)(2,1)S(1)}, bf16[8,96,128]{2,1,0:T(8,128)(2,1)S(1)}, u32[]{:S(2)}, u32[]{:S(2)}) collective-permute-start(bf16[8,96,128]{2,1,0:T(8,128)(2,1)S(1)} %slice.4), channel_id=1, source_target_pairs={{0,64},{1,65},{2,66},{3,67},{4,68},{5,69},{6,70},{7,71},{8,72},{9,... | collective-permute-start | bytes 589832 | tf_op jit(solution)/shard_map/ppermute | solution.py:294
  55.7 0.0 copy-done
  55.7 0.0 copy-done.1
  55.7 3.4 %main_part.1 = (bf16[3072,128]{1,0:T(8,128)(2,1)S(1)}, f32[48,128]{1,0:T(8,128)S(1)}, bf16[8,128,384]{2,1,0:T(8,128)(2,1)S(1)}) custom-call(s32[54]{0:T(128)S(1)} %copy-done.1, f32[8,32]{1,0:T(8,128)S(1)} %bitcast.13, bf16[64,152,128]{2,1,0:T(8,128)(2,1)S(1)} %all_to_all.10.got_ref), custom_call_target="tpu_custom_call" | custom-call | flops 2000000000 | bytes 16000000 | tf_op jit(solution)/shard_map/main_part/pallas_call | solution.py:241
  59.1 0.4 collective-permute-done.halo_ref
  59.5 0.9 %first_part.1 = (bf16[3072,128]{1,0:T(8,128)(2,1)S(1)}, bf16[8,128,384]{2,1,0:T(8,128)(2,1)S(1)}) custom-call(f32[48,128]{1,0:T(8,128)S(1)} %get-tuple-element.9.bias_ref, bf16[8,96,128]{2,1,0:T(8,128)(2,1)S(1)} %collective-permute-done.halo_ref, bf16[8,128,384]{2,1,0:T(8,128)(2,1)S(1)} %get-tuple-element.10.own_ref, ...), custom_call_target="tpu_custom_call", output_to_operand_aliasing={{1}: (2, {}), {0}: (3, {})} | custom-call | tf_op jit(solution)/shard_map/first_part/pallas_call | solution.py:265
  60.4 25.1 %all_to_all.11 = bf16[64,48,128]{2,1,0:T(8,128)(2,1)S(1)} all-to-all(bf16[64,48,128]{2,1,0:T(8,128)(2,1)S(1)} %bitcast.12), channel_id=1, replica_groups={{0,1,2,3,4,5,6,7,8,9,10,11,12,13,14,15,16,17,18,19,20,21,22,23,24,25,26..., dimensions={0} | all-to-all | bytes 1572864 | tf_op jit(solution)/shard_map/all_to_all | solution.py:277
  85.5 1.1 %copy.11 = bf16[8,8,6,8,128]{4,3,1,0,2:T(8,128)(2,1)} copy(bf16[8,8,6,8,128]{4,3,2,1,0:T(8,128)(2,1)S(1)} %bitcast.15) | data formatting | bytes 1572864 | tf_op jit(solution)/shard_map/reshape | solution.py:298
  (1 shorter events, 0.0 us)
Async XLA Ops:
  6.5 49.2 %copy-start = (f32[32,8]{0,1:T(8,128)S(1)}, f32[32,8]{0,1:T(8,128)}, u32[]{:S(2)}) copy-start(f32[32,8]{0,1:T(8,128)} %param.10) | copy-start | bytes 3076
  6.5 49.2 %copy-start.1 = (s32[54]{0:T(128)S(1)}, s32[54]{0:T(128)}, u32[]{:S(2)}) copy-start(s32[54]{0:T(128)} %bucket_ref.1) | copy-start | bytes 652
  50.8 8.7 %collective-permute-start = (bf16[8,96,128]{2,1,0:T(8,128)(2,1)S(1)}, bf16[8,96,128]{2,1,0:T(8,128)(2,1)S(1)}, u32[]{:S(2)}, u32[]{:S(2)}) collective-permute-start(bf16[8,96,128]{2,1,0:T(8,128)(2,1)S(1)} %slice.4), channel_id=1, source_target_pairs={{0,64},{1,65},{2,66},{3,67},{4,68},{5,69},{6,70},{7,71},{8,72},{9,... | collective-permute-start | bytes 589832 | tf_op jit(solution)/shard_map/ppermute | solution.py:294

commit v2 on v1

--- a/solution.py
+++ b/solution.py
@@ -156,10 +156,10 @@
     return jnp.where(seen > 0.5, base, NEG)
 
 
-def score(held, start, bias):
+def score(held, start, bias, tokens=range(ROWS)):
     first = start + CHUNK - KEYS
     scores = []
-    for s in range(0, ROWS, 2):
+    for s in tokens[::2]:
         q = jnp.concatenate([held[t, start : start + CHUNK, 2 * HEAD :] for t in (s, s + 1)], axis=0)
         k = jnp.concatenate([held[t, first : first + KEYS, 0:HEAD] for t in (s, s + 1)], axis=0)
         both = lax.dot_general(q, k, (((1,), (1,)), ((), ())), preferred_element_type=jnp.float32)
@@ -167,15 +167,15 @@
     return jnp.stack(scores, axis=0) * (HEAD**-0.5) + bias[None]
 
 
-def mix(held, start, scores):
+def mix(held, start, scores, tokens=range(ROWS)):
     first = start + CHUNK - KEYS
     expo = jnp.exp(scores - jnp.max(scores, axis=2, keepdims=True))
     weights = expo * (1.0 / jnp.sum(expo, axis=2, keepdims=True))
     weights = weights.astype(jnp.bfloat16)
     mixed = []
-    for s in range(0, ROWS, 2):
+    for n, s in enumerate(tokens[::2]):
         v = jnp.concatenate([held[t, first : first + KEYS, HEAD : 2 * HEAD] for t in (s, s + 1)], axis=1)
-        both = jnp.dot(weights[s : s + 2].reshape(2 * CHUNK, KEYS), v, preferred_element_type=jnp.float32)
+        both = jnp.dot(weights[2 * n : 2 * n + 2].reshape(2 * CHUNK, KEYS), v, preferred_element_type=jnp.float32)
         both = both.astype(jnp.bfloat16)
         mixed += [both[0:CHUNK, 0:HEAD], both[CHUNK:, HEAD:]]
     return mixed
@@ -258,7 +258,11 @@
     swap = swap_matrix(PIECE, ROWS, False)
     back = swap_matrix(PIECE, ROWS, True)
     turn_in(held, swap, halo_ref, slice(0, SPAN), 2, KEYS - 2 * CHUNK)
-    turn_out(out_ref, back, attend(held, KEYS - CHUNK, bias_ref[...]), 0)
+    bias = bias_ref[...]
+    halves = [range(0, ROWS // 2), range(ROWS // 2, ROWS)]
+    scores = [score(held, KEYS - CHUNK, bias, tokens) for tokens in halves]
+    mixed = [mix(held, KEYS - CHUNK, part, tokens) for part, tokens in zip(scores, halves)]
+    turn_out(out_ref, back, mixed[0] + mixed[1], 0)
 
 
 def first_part(bias, halo, own, rest):
@@ -273,6 +277,38 @@
     )(bias, halo, own, rest)[0]
 
 
+def unpack_kernel(got_ref, out_hbm, out_ref, sems):
+    stores = []
+    for two in range(FR // 2):
+        for head in range(HEADS):
+            tiles = [
+                got_ref[group * HEADS + head, two * 2 * ROWS : (two + 1) * 2 * ROWS, :].astype(jnp.float32)
+                for group in range(got_ref.shape[0] // HEADS)
+            ]
+            for half in range(2):
+                rows = jnp.concatenate([t[half * ROWS : (half + 1) * ROWS] for t in tiles], axis=0)
+                out_ref[2 * two + half, :, head * HEAD : (head + 1) * HEAD] = rows.astype(jnp.bfloat16)
+        span = slice(2 * two, 2 * two + 2)
+        store = pltpu.make_async_copy(out_ref.at[span], out_hbm.at[span], sems.at[two])
+        store.start()
+        stores.append(store)
+    for store in stores:
+        store.wait()
+
+
+def unpack(got):
+    shape = (FR, got.shape[0] // HEADS * ROWS, HEADS * HEAD)
+    return pl.pallas_call(
+        unpack_kernel,
+        in_specs=[VMEM],
+        out_specs=pl.BlockSpec(memory_space=pl.ANY),
+        out_shape=jax.ShapeDtypeStruct(shape, got.dtype),
+        scratch_shapes=[pltpu.VMEM(shape, jnp.bfloat16), pltpu.SemaphoreType.DMA((FR // 2,))],
+        compiler_params=pltpu.CompilerParams(vmem_limit_bytes=40 * 1024 * 1024),
+        name="unpack",
+    )(got)
+
+
 def exchange(array, groups):
     return lax.all_to_all(array, ("inner", "outer"), 0, 0, tiled=True, axis_index_groups=groups)
 
@@ -281,7 +317,7 @@
     n_outer = lax.axis_size("outer")
     n_blocks = lax.axis_size("inner") * n_outer
     groups = [list(range(g, g + GROUP)) for g in range(0, n_blocks, GROUP)]
-    spatial, width = frames.shape[2:]
+    width = frames.shape[3]
 
     sent = prep(
         frames.reshape(-1, width),
@@ -295,8 +331,7 @@
     rest, bias, own = main_part(bucket_table, bias_table.T, got)
     mixed = first_part(bias, halo, own, rest)
     out = exchange(mixed.reshape(GROUP, CHUNK, HEAD), groups)
-    out = out.reshape(spatial // ROWS, HEADS, FR, ROWS, HEAD)
-    return out.transpose(2, 0, 3, 1, 4).reshape(queries.shape)
+    return unpack(out).reshape(queries.shape)
 
 
 def solution(mesh):

time: 86.9 us -> 86.7 us (level)
  local copies, waits for them, and re-layouts: 1.13 us -> 0.03 us
  Pallas kernels: 10.8 us -> 11.7 us
    reshape x1 -> x0, local copies, waits for them, and re-layouts: 1.1 us -> none  [on_device(): out = out.reshape(spatial // ROWS, HEADS, FR, ROWS, HEAD)]
    pallas_call x0 -> x1, Pallas kernels: none -> 0.96 us  [unpack(): pl.pallas_call(unpack_kernel, in_specs=[VMEM], out_specs=pl.BlockSpec(mem...]
where the time goes in v2:
time: 86.7 us; the launch traced here: 86.5 us
  blocking collectives  69.3 us (80%)
  Pallas kernels  11.7 us (13%)
  starting transfers between devices  4.91 us (6%)
    all_to_all x2, blocking collectives, exchange(): lax.all_to_all(array, ('inner', 'outer'), 0, 0, tiled=True, axis_index_gr...  69.3 us
    pallas_call x1, Pallas kernels, prep(): pl.pallas_call(prep_kernel, in_specs=[any_] * 4, out_specs=any_, out_shap...  6.53 us
    ppermute x1, starting transfers between devices, on_device(): lax.ppermute(got[GROUP - SPAN:, :2 * CHUNK, :], ('inner', 'outer'), perm)  4.91 us
    pallas_call x1, Pallas kernels, main_part(): pl.pallas_call(main_kernel, in_specs=[SMEM, SMEM, VMEM], out_specs=[VMEM]...  3.38 us
  transfers between devices with their start and end apart: 1, of which 1 were waited for; matrix products, arithmetic and copies ran while one was open for 0% of the time, Pallas kernels for 4%

profile of v2, /device:TPU:1, one launch (start us, length us, event | category | flops | bytes accessed | tf_op | source)
XLA Modules:
  0.0 86.5 jit_solution(8615391574533757851)
XLA Ops:
  0.0 6.5 %prep.1 = bf16[8,8,152,128]{3,2,1,0:T(8,128)(2,1)} custom-call(s32[9]{0:T(128)} %bitcast.12, bf16[384,2048]{1,0:T(8,128)(2,1)} %bitcast.10, bf16[2048,2048]{1,0:T(8,128)(2,1)} %w_hbm.1, bf16[384,1024]{1,0:T(8,128)(2,1)} %bitcast.11), custom_call_target="tpu_custom_call" | custom-call | tf_op jit(solution)/shard_map/prep/pallas_call | solution.py:115
  6.5 0.0 copy-start
  6.5 0.0 copy-start.1
  6.6 44.2 %all_to_all.10.got_ref = bf16[64,152,128]{2,1,0:T(8,128)(2,1)S(1)} all-to-all(bf16[64,152,128]{2,1,0:T(8,128)(2,1)} %bitcast.9), channel_id=1, replica_groups={{0,1,2,3,4,5,6,7,8,9,10,11,12,13,14,15,16,17,18,19,20,21,22,23,24,25,26..., dimensions={0} | all-to-all | bytes 4980736 | tf_op jit(solution)/shard_map/all_to_all | solution.py:313
  50.8 4.9 %collective-permute-start = (bf16[8,96,128]{2,1,0:T(8,128)(2,1)S(1)}, bf16[8,96,128]{2,1,0:T(8,128)(2,1)S(1)}, u32[]{:S(2)}, u32[]{:S(2)}) collective-permute-start(bf16[8,96,128]{2,1,0:T(8,128)(2,1)S(1)} %slice.4), channel_id=1, source_target_pairs={{0,64},{1,65},{2,66},{3,67},{4,68},{5,69},{6,70},{7,71},{8,72},{9,... | collective-permute-start | bytes 589832 | tf_op jit(solution)/shard_map/ppermute | solution.py:330
  55.7 0.0 copy-done
  55.7 0.0 copy-done.1
  55.7 3.4 %main_part.1 = (bf16[3072,128]{1,0:T(8,128)(2,1)S(1)}, f32[48,128]{1,0:T(8,128)S(1)}, bf16[8,128,384]{2,1,0:T(8,128)(2,1)S(1)}) custom-call(s32[54]{0:T(128)S(1)} %copy-done.1, f32[8,32]{1,0:T(8,128)S(1)} %bitcast.8, bf16[64,152,128]{2,1,0:T(8,128)(2,1)S(1)} %all_to_all.10.got_ref), custom_call_target="tpu_custom_call" | custom-call | flops 2000000000 | bytes 16000000 | tf_op jit(solution)/shard_map/main_part/pallas_call | solution.py:241
  59.1 0.4 collective-permute-done.halo_ref
  59.5 0.9 %first_part.1 = (bf16[3072,128]{1,0:T(8,128)(2,1)S(1)}, bf16[8,128,384]{2,1,0:T(8,128)(2,1)S(1)}) custom-call(f32[48,128]{1,0:T(8,128)S(1)} %get-tuple-element.9.bias_ref, bf16[8,96,128]{2,1,0:T(8,128)(2,1)S(1)} %collective-permute-done.halo_ref, bf16[8,128,384]{2,1,0:T(8,128)(2,1)S(1)} %get-tuple-element.10.own_ref, ...), custom_call_target="tpu_custom_call", output_to_operand_aliasing={{1}: (2, {}), {0}: (3, {})} | custom-call | tf_op jit(solution)/shard_map/first_part/pallas_call | solution.py:269
  60.4 25.1 %all_to_all.11.got_ref = bf16[64,48,128]{2,1,0:T(8,128)(2,1)S(1)} all-to-all(bf16[64,48,128]{2,1,0:T(8,128)(2,1)S(1)} %bitcast.7), channel_id=1, replica_groups={{0,1,2,3,4,5,6,7,8,9,10,11,12,13,14,15,16,17,18,19,20,21,22,23,24,25,26..., dimensions={0} | all-to-all | bytes 1572864 | tf_op jit(solution)/shard_map/all_to_all | solution.py:313
  85.5 1.0 %unpack.1 = bf16[6,64,1024]{2,1,0:T(8,128)(2,1)} custom-call(bf16[64,48,128]{2,1,0:T(8,128)(2,1)S(1)} %all_to_all.11.got_ref), custom_call_target="tpu_custom_call" | custom-call | tf_op jit(solution)/shard_map/unpack/pallas_call | solution.py:301
  (1 shorter events, 0.0 us)
Async XLA Ops:
  6.5 49.2 %copy-start = (f32[32,8]{0,1:T(8,128)S(1)}, f32[32,8]{0,1:T(8,128)}, u32[]{:S(2)}) copy-start(f32[32,8]{0,1:T(8,128)} %param.10) | copy-start | bytes 3076
  6.5 49.2 %copy-start.1 = (s32[54]{0:T(128)S(1)}, s32[54]{0:T(128)}, u32[]{:S(2)}) copy-start(s32[54]{0:T(128)} %bucket_ref.1) | copy-start | bytes 652
  50.8 8.7 %collective-permute-start = (bf16[8,96,128]{2,1,0:T(8,128)(2,1)S(1)}, bf16[8,96,128]{2,1,0:T(8,128)(2,1)S(1)}, u32[]{:S(2)}, u32[]{:S(2)}) collective-permute-start(bf16[8,96,128]{2,1,0:T(8,128)(2,1)S(1)} %slice.4), channel_id=1, source_target_pairs={{0,64},{1,65},{2,66},{3,67},{4,68},{5,69},{6,70},{7,71},{8,72},{9,... | collective-permute-start | bytes 589832 | tf_op jit(solution)/shard_map/ppermute | solution.py:330

commit v3 on v2

--- a/solution.py
+++ b/solution.py
@@ -48,8 +48,9 @@
         )
     q_load = pltpu.make_async_copy(q_hbm, q, q_sem)
     mask_load = pltpu.make_async_copy(mask_hbm, mask_ref, mask_sem)
-    for load in loads[0] + loads[1]:
-        load.start()
+    for slab in range(2):
+        for load in loads[slab]:
+            load.start(priority=slab)
     mask_load.start()
     spatial = x.shape[0] // FR
 
@@ -79,7 +80,7 @@
             load.wait()
         if slab + 2 < SLABS:
             for load in loads[slab + 2]:
-                load.start()
+                load.start(priority=slab % 2)
         if slab == 0:
             q_load.start()
         if slab == SLABS - 1:

time: 86.7 us -> 86.7 us (level)
  no operation moved by 1% of the time
where the time goes in v3:
time: 86.7 us; the launch traced here: 86.5 us
  blocking collectives  69.3 us (80%)
  Pallas kernels  11.7 us (13%)
  starting transfers between devices  4.91 us (6%)
    all_to_all x2, blocking collectives, exchange(): lax.all_to_all(array, ('inner', 'outer'), 0, 0, tiled=True, axis_index_gr...  69.3 us
    pallas_call x1, Pallas kernels, prep(): pl.pallas_call(prep_kernel, in_specs=[any_] * 4, out_specs=any_, out_shap...  6.52 us
    ppermute x1, starting transfers between devices, on_device(): lax.ppermute(got[GROUP - SPAN:, :2 * CHUNK, :], ('inner', 'outer'), perm)  4.91 us
    pallas_call x1, Pallas kernels, main_part(): pl.pallas_call(main_kernel, in_specs=[SMEM, SMEM, VMEM], out_specs=[VMEM]...  3.38 us
  transfers between devices with their start and end apart: 1, of which 1 were waited for; matrix products, arithmetic and copies ran while one was open for 0% of the time, Pallas kernels for 4%

profile of v3, /device:TPU:1, one launch (start us, length us, event | category | flops | bytes accessed | tf_op | source)
XLA Modules:
  0.0 86.5 jit_solution(13432226343088504067)
XLA Ops:
  0.0 6.5 %prep.1 = bf16[8,8,152,128]{3,2,1,0:T(8,128)(2,1)} custom-call(s32[9]{0:T(128)} %bitcast.12, bf16[384,2048]{1,0:T(8,128)(2,1)} %bitcast.10, bf16[2048,2048]{1,0:T(8,128)(2,1)} %w_hbm.1, bf16[384,1024]{1,0:T(8,128)(2,1)} %bitcast.11), custom_call_target="tpu_custom_call" | custom-call | tf_op jit(solution)/shard_map/prep/pallas_call | solution.py:116
  6.5 0.0 copy-start
  6.5 0.0 copy-start.1
  6.6 44.2 %all_to_all.10.got_ref = bf16[64,152,128]{2,1,0:T(8,128)(2,1)S(1)} all-to-all(bf16[64,152,128]{2,1,0:T(8,128)(2,1)} %bitcast.9), channel_id=1, replica_groups={{0,1,2,3,4,5,6,7,8,9,10,11,12,13,14,15,16,17,18,19,20,21,22,23,24,25,26..., dimensions={0} | all-to-all | bytes 4980736 | tf_op jit(solution)/shard_map/all_to_all | solution.py:314
  50.8 4.9 %collective-permute-start = (bf16[8,96,128]{2,1,0:T(8,128)(2,1)S(1)}, bf16[8,96,128]{2,1,0:T(8,128)(2,1)S(1)}, u32[]{:S(2)}, u32[]{:S(2)}) collective-permute-start(bf16[8,96,128]{2,1,0:T(8,128)(2,1)S(1)} %slice.4), channel_id=1, source_target_pairs={{0,64},{1,65},{2,66},{3,67},{4,68},{5,69},{6,70},{7,71},{8,72},{9,... | collective-permute-start | bytes 589832 | tf_op jit(solution)/shard_map/ppermute | solution.py:331
  55.7 0.0 copy-done
  55.7 0.0 copy-done.1
  55.7 3.4 %main_part.1 = (bf16[3072,128]{1,0:T(8,128)(2,1)S(1)}, f32[48,128]{1,0:T(8,128)S(1)}, bf16[8,128,384]{2,1,0:T(8,128)(2,1)S(1)}) custom-call(s32[54]{0:T(128)S(1)} %copy-done.1, f32[8,32]{1,0:T(8,128)S(1)} %bitcast.8, bf16[64,152,128]{2,1,0:T(8,128)(2,1)S(1)} %all_to_all.10.got_ref), custom_call_target="tpu_custom_call" | custom-call | flops 2000000000 | bytes 16000000 | tf_op jit(solution)/shard_map/main_part/pallas_call | solution.py:242
  59.1 0.4 collective-permute-done.halo_ref
  59.5 0.9 %first_part.1 = (bf16[3072,128]{1,0:T(8,128)(2,1)S(1)}, bf16[8,128,384]{2,1,0:T(8,128)(2,1)S(1)}) custom-call(f32[48,128]{1,0:T(8,128)S(1)} %get-tuple-element.9.bias_ref, bf16[8,96,128]{2,1,0:T(8,128)(2,1)S(1)} %collective-permute-done.halo_ref, bf16[8,128,384]{2,1,0:T(8,128)(2,1)S(1)} %get-tuple-element.10.own_ref, ...), custom_call_target="tpu_custom_call", output_to_operand_aliasing={{1}: (2, {}), {0}: (3, {})} | custom-call | tf_op jit(solution)/shard_map/first_part/pallas_call | solution.py:270
  60.4 25.1 %all_to_all.11.got_ref = bf16[64,48,128]{2,1,0:T(8,128)(2,1)S(1)} all-to-all(bf16[64,48,128]{2,1,0:T(8,128)(2,1)S(1)} %bitcast.7), channel_id=1, replica_groups={{0,1,2,3,4,5,6,7,8,9,10,11,12,13,14,15,16,17,18,19,20,21,22,23,24,25,26..., dimensions={0} | all-to-all | bytes 1572864 | tf_op jit(solution)/shard_map/all_to_all | solution.py:314
  85.5 1.0 %unpack.1 = bf16[6,64,1024]{2,1,0:T(8,128)(2,1)} custom-call(bf16[64,48,128]{2,1,0:T(8,128)(2,1)S(1)} %all_to_all.11.got_ref), custom_call_target="tpu_custom_call" | custom-call | tf_op jit(solution)/shard_map/unpack/pallas_call | solution.py:302
  (1 shorter events, 0.0 us)
Async XLA Ops:
  6.5 49.2 %copy-start = (f32[32,8]{0,1:T(8,128)S(1)}, f32[32,8]{0,1:T(8,128)}, u32[]{:S(2)}) copy-start(f32[32,8]{0,1:T(8,128)} %param.10) | copy-start | bytes 3076
  6.5 49.2 %copy-start.1 = (s32[54]{0:T(128)S(1)}, s32[54]{0:T(128)}, u32[]{:S(2)}) copy-start(s32[54]{0:T(128)} %bucket_ref.1) | copy-start | bytes 652
  50.8 8.7 %collective-permute-start = (bf16[8,96,128]{2,1,0:T(8,128)(2,1)S(1)}, bf16[8,96,128]{2,1,0:T(8,128)(2,1)S(1)}, u32[]{:S(2)}, u32[]{:S(2)}) collective-permute-start(bf16[8,96,128]{2,1,0:T(8,128)(2,1)S(1)} %slice.4), channel_id=1, source_target_pairs={{0,64},{1,65},{2,66},{3,67},{4,68},{5,69},{6,70},{7,71},{8,72},{9,... | collective-permute-start | bytes 589832 | tf_op jit(solution)/shard_map/ppermute | solution.py:331
